TPU v7x, 32 devices: a whole 2x2x4 slice. The times are simulated.
32 devices in a mesh: col: 16 (over z, x, core), row: 2 (over y).
Axes of the slice: x: 2, y: 2, z: 4, core: 2. Of those that a mesh axis runs over, the one named last changes fastest.
Arguments:
- matrix: float32 [8, 256, 1, 2048], P(None, 'row', None, 'col'), may hold values from -1 to 5, as said below
- inverse_factors: float32 [2, 512, 512], replicated, may hold values from -1 to 1, as said below
Outputs:
- factored: float32 [8, 256, 1, 2048], P(None, 'row', None, 'col')
Inputs may be any that keep to these rules, and one draw needn't show every extreme that they name: matrix holds a symmetric matrix. Each inverse_factors[k] is lower triangular with a positive diagonal; it is given independently of matrix.
All inputs are finite; a program needn't handle non-finite values.
Results may differ from a plain program's by a relative error of at most 0.0001.
Values sent between devices are 32-bit elements; how exact they have to be, the bound alone decides.
A program may use at most 64 MiB of HBM per device.

v0:
```python
import jax
import jax.numpy as jnp
from jax import lax
from jax.sharding import PartitionSpec as P


def broadcast(x, axis, root):
    mine = lax.axis_index(axis) == root
    return lax.psum(jnp.where(mine, x, jnp.zeros_like(x)), axis)


def exact_dot(left_side, right_side):
    return jnp.dot(
        left_side, right_side, precision=lax.Precision.HIGHEST, preferred_element_type=jnp.float32
    )


def shards(matrix, inverse_factors):
    col_count = lax.axis_size("col")
    row_count = lax.axis_size("row")
    col_index = lax.axis_index("col")
    row_index = lax.axis_index("row")
    row_blocks, block_cols, cycles, _ = matrix.shape
    panel_width = inverse_factors.shape[1]
    per_panel = panel_width // block_cols
    local_rows = row_blocks * block_cols
    square_view = matrix.reshape(local_rows, cycles * block_cols)
    global_rows = (
        (jnp.arange(row_blocks)[:, None] * row_count + row_index) * block_cols
        + jnp.arange(block_cols)[None, :]
    ).reshape(-1)
    take_index = (jnp.arange(cycles) * col_count + col_index) // row_count
    row_root = col_index % row_count

    def masked(factor_cols, offset):
        return jnp.where(global_rows[:, None] >= offset, factor_cols, 0.0)

    current = square_view
    for panel in range(2):
        factor = inverse_factors[panel]
        pieces = [
            broadcast(current, "col", panel * per_panel + member) for member in range(per_panel)
        ]
        factor_cols = exact_dot(jnp.concatenate(pieces, axis=1), factor.T)
        trailing = masked(factor_cols, (panel + 1) * panel_width)
        blocked = trailing.reshape(row_blocks, block_cols, panel_width)
        picked = jnp.take(blocked, take_index, axis=0).reshape(cycles * block_cols, panel_width)
        gathered = lax.all_gather(picked, "row", axis=0, tiled=True)
        column_part = lax.dynamic_slice_in_dim(
            gathered, row_root * picked.shape[0], picked.shape[0], 0
        )
        current = current - exact_dot(trailing, column_part.T)
        place_factor_cols = masked(factor_cols, panel * panel_width)
        offset_id = col_index - panel * per_panel
        inside = (offset_id >= 0) & (offset_id < per_panel)
        position = jnp.clip(offset_id, 0, per_panel - 1)
        chosen = lax.dynamic_slice_in_dim(place_factor_cols, position * block_cols, block_cols, 1)
        leading = jnp.where(inside, chosen, current)
        current = jnp.concatenate([leading, current[:, block_cols:]], axis=1)
    return current.reshape(row_blocks, block_cols, cycles, block_cols)


def solution(mesh):
    return jax.shard_map(
        shards,
        mesh=mesh,
        in_specs=(P(None, "row", None, "col"), P()),
        out_specs=P(None, "row", None, "col"),
        check_vma=False,
    )
```

profile of v0, /device:TPU:0, one launch (start us, length us, event | category | flops | bytes accessed | tf_op | source)
XLA Modules:
  0.0 248.7 jit_solution(13387208267535099362)
XLA Ops:
  6.5 0.0 all-reduce.7.cloned.1.call-start
  6.5 0.0 copy-start
  6.5 2.6 %broadcast_select_fusion.9 = (f32[1024,128]{1,0:T(8,128)}, f32[1024,128]{1,0:T(8,128)}, f32[1024,128]{1,0:T(8,128)}, f32[1024,128]{1,0:T(8,128)}) fusion(f32[1024,128]{1,0:T(8,128)} %bitcast.39, pred[]{:T(512)S(6)} %eq.27, pred[]{:T(512)S(6)} %eq.30, pred[]{:T(512)S(6)} %eq.29, pred[]{:T(512)S(6)} %eq.28), kind=kLoop, calls=%fused_computation.41 | loop fusion | flops 524288 | bytes 2621444 | tf_op jit(solution)/shard_map/jit(_where)/select_n | solution.py:9
  9.1 0.0 all-reduce.7.cloned.1.call-update
  9.1 0.0 all-reduce.5.cloned.1.call-start
  9.2 0.1 fusion.31
  9.3 103.0 %all-reduce.7.cloned.1.call-done = (f32[1024,128]{1,0:T(8,128)}, f32[1024,128]{1,0:T(8,128)}, f32[1024,128]{1,0:T(8,128)}, f32[1024,128]{1,0:T(8,128)}) async-done(((f32[1024,128]{1,0:T(8,128)}, f32[1024,128]{1,0:T(8,128)}, f32[1024,128]{1,0:T(8,128)}, f32[1024,128]{1,0:T(8,128)}), (f32[1024,128]{1,0:T(8,128)}, f32[1024,128]{1,0:T(8,128)}, f32[1024,128]{1,0:T(8,128)}, ...) | async-done | bytes 2097168 | tf_op jit(solution)/shard_map/psum | solution.py:9
  112.4 0.0 copy-done
  112.4 0.0 copy-start.1
  112.4 5.0 %broadcast_select_fusion = (f32[1024,512]{1,0:T(8,128)S(1)}, f32[1024,512]{1,0:T(8,128)S(1)}) fusion(pred[1024]{0:T(1024)(128)(4,1)S(1)} %get-tuple-element.35, f32[2,512,512]{2,1,0:T(8,128)S(1)} %copy-done, f32[1024,128]{1,0:T(8,128)} %get-tuple-element.21, f32[1024,128]{1,0:T(8,128)} %get-tuple-element.22, f32[1024,128]{1,0:T(8,128)} %get-tuple-element.23, ...), kind=kOutput, calls=%fused_computation.23 | convolution fusion | flops 3223322624 | bytes 7341056 | tf_op jit(solution)/shard_map/dot_general | solution.py:13
  117.5 8.0 %all-gather = f32[1,256,512]{2,1,0:T(8,128)S(1)} all-gather(f32[1,128,512]{2,1,0:T(8,128)S(1)} %dynamic-slice_select_fusion.3), channel_id=2, replica_groups=mesh['col'=16,'row'=2] {'row'}, dimensions={1}, use_global_device_ids=true | all-gather | bytes 786432 | tf_op jit(solution)/shard_map/all_gather | solution.py:48
  125.5 0.0 copy-done.1
  125.5 3.2 %broadcast_select_fusion.5 = (f32[1024,128]{1,0:T(8,128)}, f32[1024,128]{1,0:T(8,128)}, f32[1024,128]{1,0:T(8,128)}, f32[1024,128]{1,0:T(8,128)}, f32[1024,128]{1,0:T(8,128)S(1)}) fusion(pred[]{:T(512)S(6)} %eq.26, pred[]{:T(512)S(6)} %eq.33, pred[]{:T(512)S(6)} %eq.32, pred[]{:T(512)S(6)} %eq.31, f32[1024,128]{1,0:T(8,128)S(1)} %bitcast.40, ...), kind=kOutput, calls=%fused_computation.37 | convolution fusion | flops 806223872 | bytes 6030349 | tf_op jit(solution)/shard_map/dot_general | solution.py:13
  128.6 0.0 all-reduce.5.cloned.1.call-update
  128.7 97.5 %all-reduce.5.cloned.1.call-done = (f32[1024,128]{1,0:T(8,128)}, f32[1024,128]{1,0:T(8,128)}, f32[1024,128]{1,0:T(8,128)}, f32[1024,128]{1,0:T(8,128)}) async-done(((f32[1024,128]{1,0:T(8,128)}, f32[1024,128]{1,0:T(8,128)}, f32[1024,128]{1,0:T(8,128)}, f32[1024,128]{1,0:T(8,128)}), (f32[1024,128]{1,0:T(8,128)}, f32[1024,128]{1,0:T(8,128)}, f32[1024,128]{1,0:T(8,128)}, ...) | async-done | bytes 2097168 | tf_op jit(solution)/shard_map/psum | solution.py:9
  226.2 5.0 %broadcast_select_fusion.1 = (f32[1024,512]{1,0:T(8,128)S(1)}, f32[1024,512]{1,0:T(8,128)S(1)}) fusion(pred[1024]{0:T(1024)(128)(4,1)S(1)} %get-tuple-element.33, f32[2,512,512]{2,1,0:T(8,128)S(1)} %copy-done, f32[1024,128]{1,0:T(8,128)} %get-tuple-element.17, f32[1024,128]{1,0:T(8,128)} %get-tuple-element.18, f32[1024,128]{1,0:T(8,128)} %get-tuple-element.19, ...), kind=kOutput, calls=%fused_computation.24 | convolution fusion | flops 3223322624 | bytes 7341056 | tf_op jit(solution)/shard_map/dot_general | solution.py:13
  231.2 8.0 %all-gather.1 = f32[1,256,512]{2,1,0:T(8,128)S(1)} all-gather(f32[1,128,512]{2,1,0:T(8,128)S(1)} %dynamic-slice_select_fusion.2), channel_id=3, replica_groups=mesh['col'=16,'row'=2] {'row'}, dimensions={1}, use_global_device_ids=true | all-gather | bytes 786432 | tf_op jit(solution)/shard_map/all_gather | solution.py:48
  239.2 2.6 %fusion.16 = f32[1024,128]{1,0:T(8,128)} fusion(f32[1024,128]{1,0:T(8,128)S(1)} %get-tuple-element.38, f32[1024,512]{1,0:T(8,128)S(1)} %get-tuple-element.39, f32[1024,512]{1,0:T(8,128)S(1)} %get-tuple-element.40, s32[]{:T(128)S(6)} %select_n.137, f32[1,256,512]{2,1,0:T(8,128)S(1)} %all-gather.1, s32[]{:T(128)S(6)} %select_n.127, ...), kind=kOutput, calls=%fused_computation.17 | convolution fusion | flops 805699584 | bytes 3933193 | tf_op jit(solution)/shard_map/dot_general | solution.py:13
  (3 shorter events, 0.1 us)
Async XLA Ops:
  6.5 105.8 %all-reduce.7.cloned.1.call-start = ((), (), s32[]{:S(2)}) async-start(), calls=%async_computation.1 | async-start | bytes 4194304 | tf_op jit(solution)/shard_map/psum | solution.py:9
  6.5 105.8 %copy-start = (f32[2,512,512]{2,1,0:T(8,128)S(1)}, f32[2,512,512]{2,1,0:T(8,128)}, u32[]{:S(2)}) copy-start(f32[2,512,512]{2,1,0:T(8,128)} %param.5) | copy-start | bytes 6291460
  9.1 217.1 %all-reduce.5.cloned.1.call-start = ((), (), s32[]{:S(2)}) async-start(), calls=%async_computation | async-start | bytes 4194304 | tf_op jit(solution)/shard_map/psum | solution.py:9
  112.4 13.1 %copy-start.1 = (f32[8,128,1,128]{3,2,1,0:T(1,128)S(1)}, f32[8,128,1,128]{3,2,1,0:T(1,128)}, u32[]{:S(2)}) copy-start(f32[8,128,1,128]{3,2,1,0:T(1,128)} %param.4) | copy-start | bytes 1572868
Sparse Core Ops, SparseCore 0:
  11.3 101.0 all-reduce.6
  128.8 97.3 all-reduce.4
where the time goes:
time: 249 us
  waiting for transfers between devices  201 us (81%)
  blocking collectives  16 us (6%)
  matrix products  15.8 us (6%)
  between operations  13.5 us (5%)
  other arithmetic  2.7 us (1%)
    psum x2, waiting for transfers between devices, broadcast(): return lax.psum(jnp.where(mine, x, jnp.zeros_like(x)), axis)  201 us
    all_gather x2, blocking collectives, shards(): gathered = lax.all_gather(picked, 'row', axis=0, tiled=True)  16 us
    dot_general x4, matrix products, exact_dot(): jnp.dot(left_side, right_side, precision=lax.Precision.HIGHEST, preferred...  15.8 us
  transfers between devices with their start and end apart: 2, of which 2 were waited for; matrix products, arithmetic and copies ran while one was open for 0% of the time, Pallas kernels for 0%

commit v1 on v0

--- a/solution.py
+++ b/solution.py
@@ -1,6 +1,8 @@
 import jax
 import jax.numpy as jnp
 from jax import lax
+from jax.experimental import pallas as pl
+from jax.experimental.pallas import tpu as pltpu
 from jax.sharding import PartitionSpec as P
 
 
@@ -60,9 +62,337 @@
     return current.reshape(row_blocks, block_cols, cycles, block_cols)
 
 
+def split(value):
+    high = value.astype(jnp.bfloat16)
+    return high, (value - high.astype(jnp.float32)).astype(jnp.bfloat16)
+
+
+def dot3(left_side, right_side, right_dim=0):
+    left_high, left_low = split(left_side)
+    right_high, right_low = split(right_side)
+
+    def part(left, right):
+        return lax.dot_general(
+            left, right, (((1,), (right_dim,)), ((), ())), preferred_element_type=jnp.float32
+        )
+
+    return part(left_high, right_high) + (part(left_high, right_low) + part(left_low, right_high))
+
+
+def kernel(
+    mat, fac, out, pan, oth, colo, colf, cross, gram, first, second,
+    recv, oth_recv, col_recv, up_sem, side_sem, mate_sem, peer_sem, col_sem,
+):
+    c = lax.axis_index("col")
+    r = lax.axis_index("row")
+    z = c // 4
+    x = (c // 2) % 2
+    k = c % 2
+    own = c % 4
+    beside = own + 2 - 4 * x
+    near = own + 1 - 2 * k
+    far = beside + 1 - 2 * k
+    up = {"col": c + 4, "row": r}
+    down = {"col": c - 4, "row": r}
+    side = {"col": c + 2 - 4 * x, "row": r}
+    mate = {"col": c + 1 - 2 * k, "row": r}
+    peer = {"col": c, "row": 1 - r}
+    block = mat.shape[1]
+    width = fac.shape[1]
+    mesh_ids = pl.DeviceIdType.MESH
+
+    def greet(device):
+        pl.semaphore_signal(barrier, inc=1, device_id=device, device_id_type=mesh_ids)
+
+    def copy(src, dst, send, receive, device):
+        return pltpu.make_async_remote_copy(
+            src_ref=src, dst_ref=dst, send_sem=send, recv_sem=receive,
+            device_id=device, device_id_type=mesh_ids,
+        )
+
+    def active(q, j):
+        if q == 0:
+            return z == 0 if j == 0 else z >= 0
+        return z == 1 if j == 1 else z >= 1
+
+    def rises(q, j):
+        return z < 3 if q == 0 else (z >= 1) & (z < 3)
+
+    def climbs(q, j):
+        return j >= 1 + q
+
+    def strip(q, s, j):
+        return pan.at[q, s, pl.ds(2 * j, 2)]
+
+    def strip_copy(q, s, j, send, device):
+        return copy(strip(q, s, j), strip(q, s, j), send, recv.at[q, s, j], device)
+
+    def up_copy(q, j):
+        return strip_copy(q, own, j, up_sem.at[q, j], up)
+
+    def side_copy(q, j):
+        return strip_copy(q, own, j, side_sem.at[q, j], side)
+
+    def mate_copy(q, j, which):
+        return strip_copy(q, (own, beside)[which], j, mate_sem.at[q, j, which], mate)
+
+    def arrived(q, s, j):
+        strip_copy(q, s, j, up_sem.at[q, j], mate).wait_recv()
+
+    def peer_copy(which):
+        s = (own, beside)[which]
+        return copy(strip(0, s, 1), oth.at[s], peer_sem.at[0, which], oth_recv.at[s], peer)
+
+    def oth_copy(which):
+        s = (own, beside)[which]
+        return copy(oth.at[s], oth.at[s], peer_sem.at[1, which], oth_recv.at[s], mate)
+
+    def oth_arrived(s):
+        copy(oth.at[s], oth.at[s], peer_sem.at[1, 0], oth_recv.at[s], mate).wait_recv()
+
+    col_copy = copy(mat.at[pl.ds(0, 4)], colo, col_sem, col_recv, peer)
+
+    def lane(q, j):
+        @pl.when(active(q, j))
+        def _():
+            @pl.when(z != q)
+            def _():
+                arrived(q, own, j)
+
+            if climbs(q, j):
+                @pl.when(rises(q, j))
+                def _():
+                    up_copy(q, j).start()
+
+            side_copy(q, j).start()
+            mate_copy(q, j, 0).start()
+
+    def across(q, j):
+        @pl.when(active(q, j))
+        def _():
+            arrived(q, beside, j)
+            mate_copy(q, j, 1).start()
+
+    def complete(q, j):
+        @pl.when(active(q, j))
+        def _():
+            arrived(q, near, j)
+            arrived(q, far, j)
+
+    def rows(q, j):
+        half = [
+            jnp.concatenate([pan[q, s, 2 * j + i] for s in range(4)], axis=1) for i in range(2)
+        ]
+        return jnp.concatenate(half, axis=0)
+
+    def put(j, value):
+        out[2 * j] = value[:block]
+        out[2 * j + 1] = value[block:]
+
+    def base(j):
+        return jnp.concatenate([mat[2 * j], mat[2 * j + 1]], axis=0)
+
+    barrier = pltpu.get_barrier_semaphore()
+    greet(side)
+    greet(mate)
+    greet(peer)
+
+    @pl.when(z < 3)
+    def _():
+        greet(up)
+
+    @pl.when(z > 0)
+    def _():
+        greet(down)
+
+    for q in range(2):
+        @pl.when(z == q)
+        def _():
+            pan[q, own] = mat[...]
+
+    between = (z > 0) & (z < 3)
+
+    @pl.when(between)
+    def _():
+        pl.semaphore_wait(barrier, 5)
+
+    @pl.when(jnp.logical_not(between))
+    def _():
+        pl.semaphore_wait(barrier, 4)
+
+    chunks = [(1, 2), (0, 1), (1, 3), (0, 2), (0, 3), (1, 1), (0, 0)]
+
+    @pl.when(z == 1)
+    def _():
+        lane(1, 2)
+
+    @pl.when(z == 0)
+    def _():
+        lane(0, 1)
+        lane(0, 2)
+        lane(0, 0)
+        lane(0, 3)
+
+    @pl.when(z >= 2)
+    def _():
+        col_copy.start()
+
+    @pl.when(z >= 1)
+    def _():
+        gram[0] = dot3(fac[0].T, fac[0])
+
+    @pl.when(z >= 2)
+    def _():
+        gram[1] = dot3(fac[1].T, fac[1])
+
+    @pl.when(z >= 1)
+    def _():
+        lane(0, 1)
+        peer_copy(0).start()
+
+        @pl.when(z >= 2)
+        def _():
+            lane(1, 2)
+
+        across(0, 1)
+        peer_copy(1).start()
+        lane(1, 3)
+        across(1, 2)
+        oth_arrived(own)
+        oth_copy(0).start()
+        lane(0, 2)
+        lane(1, 1)
+        across(1, 3)
+
+        @pl.when(z >= 2)
+        def _():
+            col_copy.wait_recv()
+            for i in range(4):
+                colf[2 * i + r] = mat[i]
+                colf[2 * i + 1 - r] = colo[i]
+            first[...] = dot3(gram[0], colf[0:4].reshape(width, block))
+
+        oth_arrived(beside)
+        oth_copy(1).start()
+        across(0, 2)
+        lane(0, 3)
+        across(1, 1)
+        across(0, 3)
+
+        complete(0, 1)
+        oth_arrived(near)
+        oth_arrived(far)
+        for i in range(2):
+            for s in range(4):
+                cross[2 * i + r, :, s * block:(s + 1) * block] = pan[0, s, 2 + i]
+                cross[2 * i + 1 - r, :, s * block:(s + 1) * block] = oth[s, i]
+
+        @pl.when(z == 1)
+        def _():
+            second[...] = -fac[1, pl.ds(pl.multiple_of(own * block, block), block), :].T
+            first[...] = -dot3(cross[...].reshape(width, width).T, second[...])
+
+        @pl.when(z >= 2)
+        def _():
+            put(0, base(0))
+            lower = dot3(cross[...].reshape(width, width), first[...])
+            colf[4:8] = colf[4:8] - lower.reshape(4, block, block)
+            for i in range(2):
+                out[2 + i] = colf[4 + 2 * i + r]
+            second[...] = dot3(gram[1], colf[4:8].reshape(width, block))
+            first[...] = colf[0:4].reshape(width, block) - dot3(
+                cross[...].reshape(width, width).T, second[...]
+            )
+
+        first[...] = dot3(gram[0], first[...])
+        first_value, second_value = first[...], second[...]
+
+        @pl.when(z == 1)
+        def _():
+            put(0, jnp.zeros((2 * block, block), jnp.float32))
+            complete(1, 1)
+            put(1, -(dot3(rows(0, 1), first[...]) + dot3(rows(1, 1), second[...])))
+
+        for j in (2, 3):
+            complete(1, j)
+            complete(0, j)
+            update = dot3(rows(1, j), second_value) + dot3(rows(0, j), first_value)
+            put(j, jnp.where(z >= 2, base(j), 0.0) - update)
+
+    @pl.when(z == 0)
+    def _():
+        for j in (1, 2, 0, 3):
+            across(0, j)
+        factor = fac[0, pl.ds(pl.multiple_of(own * block, block), block), :]
+        for j in (1, 2, 0, 3):
+            complete(0, j)
+            put(j, dot3(rows(0, j), factor, 1))
+
+    for q, j in chunks:
+        @pl.when(active(q, j))
+        def _():
+            if climbs(q, j):
+                @pl.when(rises(q, j))
+                def _():
+                    up_copy(q, j).wait_send()
+            side_copy(q, j).wait_send()
+            mate_copy(q, j, 0).wait_send()
+            mate_copy(q, j, 1).wait_send()
+
+    @pl.when(z >= 1)
+    def _():
+        for which in range(2):
+            peer_copy(which).wait_send()
+            oth_copy(which).wait_send()
+
+    @pl.when(z >= 2)
+    def _():
+        col_copy.wait_send()
+
+
+def panels(matrix, inverse_factors):
+    row_blocks, block, _, _ = matrix.shape
+    width = inverse_factors.shape[1]
+    square = pltpu.VMEM((width, block), jnp.float32)
+    dma = pltpu.SemaphoreType.DMA
+    vmem = pl.BlockSpec(memory_space=pltpu.VMEM)
+    result = pl.pallas_call(
+        kernel,
+        out_shape=jax.ShapeDtypeStruct((row_blocks, block, block), jnp.float32),
+        in_specs=[vmem, vmem],
+        out_specs=vmem,
+        scratch_shapes=[
+            pltpu.VMEM((2, 4, row_blocks, block, block), jnp.float32),
+            pltpu.VMEM((4, 2, block, block), jnp.float32),
+            pltpu.VMEM((4, block, block), jnp.float32),
+            pltpu.VMEM((8, block, block), jnp.float32),
+            pltpu.VMEM((4, block, width), jnp.float32),
+            pltpu.VMEM((2, width, width), jnp.float32),
+            square,
+            square,
+            dma((2, 4, 4)),
+            dma((4,)),
+            dma,
+            dma((2, 4)),
+            dma((2, 4)),
+            dma((2, 4, 2)),
+            dma((2, 2)),
+            dma,
+        ],
+        compiler_params=pltpu.CompilerParams(
+            collective_id=0, has_side_effects=True, vmem_limit_bytes=48 * 1024 * 1024
+        ),
+        cost_estimate=pl.CostEstimate(
+            flops=2 * 10**9, bytes_accessed=4 * 2**20, transcendentals=0
+        ),
+    )(matrix.reshape(row_blocks, block, block), inverse_factors)
+    return result.reshape(matrix.shape)
+
+
 def solution(mesh):
+    small = mesh.shape["col"] == 16 and mesh.shape["row"] == 2
     return jax.shard_map(
-        shards,
+        panels if small else shards,
         mesh=mesh,
         in_specs=(P(None, "row", None, "col"), P()),
         out_specs=P(None, "row", None, "col"),

time: 249 us -> 39.7 us (0.16)
  the two profiles are of different devices: /device:TPU:0 before, /device:TPU:28 now
where the time goes in v1:
time: 39.7 us; the launch traced here: 39.5 us
  Pallas kernels  36.1 us (91%)
  local copies, waits for them, and re-layouts  3.43 us (9%)
    pallas_call x1, Pallas kernels, panels(): pl.pallas_call(kernel, out_shape=jax.ShapeDtypeStruct((row_blocks, block,...  36.1 us
    unnamed x5, local copies, waits for them, and re-layouts  3.43 us

profile of v1, /device:TPU:28, one launch (start us, length us, event | category | flops | bytes accessed | tf_op | source)
XLA Modules:
  0.0 39.5 jit_solution(5038166987578528493)
XLA Ops:
  0.0 0.0 copy-start
  0.0 1.6 %copy-done = f32[2,512,512]{2,1,0:T(8,128)S(1)} copy-done((f32[2,512,512]{2,1,0:T(8,128)S(1)}, f32[2,512,512]{2,1,0:T(8,128)}, u32[]{:S(2)}) %copy-start) | copy-done | bytes 2097176
  1.6 0.0 copy-start.1
  1.6 1.0 %copy-done.1 = f32[8,128,1,128]{3,2,1,0:T(1,128)S(1)} copy-done((f32[8,128,1,128]{3,2,1,0:T(1,128)S(1)}, f32[8,128,1,128]{3,2,1,0:T(1,128)}, u32[]{:S(2)}) %copy-start.1) | copy-done | bytes 524312
  2.6 36.1 %shard_map.28 = f32[8,128,128]{2,1,0:T(8,128)S(1)} custom-call(f32[8,128,128]{2,1,0:T(8,128)S(1)} %bitcast.5, f32[2,512,512]{2,1,0:T(8,128)S(1)} %copy-done), custom_call_target="tpu_custom_call" | custom-call | flops 2000000000 | bytes 4194304 | tf_op jit(solution)/shard_map/pallas_call | solution.py:359
  38.7 0.8 %copy.5 = f32[8,128,1,128]{3,2,1,0:T(1,128)} copy(f32[8,128,1,128]{3,2,1,0:T(1,128)S(1)} %bitcast.4) | data formatting | bytes 1048576
Async XLA Ops:
  0.0 1.6 %copy-start = (f32[2,512,512]{2,1,0:T(8,128)S(1)}, f32[2,512,512]{2,1,0:T(8,128)}, u32[]{:S(2)}) copy-start(f32[2,512,512]{2,1,0:T(8,128)} %fac.1) | copy-start | bytes 6291460
  1.6 1.0 %copy-start.1 = (f32[8,128,1,128]{3,2,1,0:T(1,128)S(1)}, f32[8,128,1,128]{3,2,1,0:T(1,128)}, u32[]{:S(2)}) copy-start(f32[8,128,1,128]{3,2,1,0:T(1,128)} %param.2) | copy-start | bytes 1572868

commit v2 on v1

--- a/solution.py
+++ b/solution.py
@@ -80,8 +80,8 @@
 
 
 def kernel(
-    mat, fac, out, pan, oth, colo, colf, cross, gram, first, second,
-    recv, oth_recv, col_recv, up_sem, side_sem, mate_sem, peer_sem, col_sem,
+    mat, fac, out, pan, oth, colf, dcol, cross, gram, first, second,
+    recv, oth_recv, col_recv, up_sem, side_sem, mate_sem, peer_sem, col_sem, strip_recv, strip_send,
 ):
     c = lax.axis_index("col")
     r = lax.axis_index("row")
@@ -112,14 +112,14 @@
 
     def active(q, j):
         if q == 0:
-            return z == 0 if j == 0 else z >= 0
-        return z == 1 if j == 1 else z >= 1
+            return (z == 0, z >= 0, z < 2, z < 2)[j]
+        return z == 1
 
     def rises(q, j):
-        return z < 3 if q == 0 else (z >= 1) & (z < 3)
+        return z < 3 if j == 1 else z == 0
 
     def climbs(q, j):
-        return j >= 1 + q
+        return q == 0 and j >= 1
 
     def strip(q, s, j):
         return pan.at[q, s, pl.ds(2 * j, 2)]
@@ -150,7 +150,49 @@
     def oth_arrived(s):
         copy(oth.at[s], oth.at[s], peer_sem.at[1, 0], oth_recv.at[s], mate).wait_recv()
 
-    col_copy = copy(mat.at[pl.ds(0, 4)], colo, col_sem, col_recv, peer)
+    def col_copy(i):
+        return copy(mat.at[i], colf.at[2 * i + r], col_sem.at[i], col_recv.at[i], peer)
+
+    turn = 4 * (5 - 2 * z)
+    turned = {"col": c + turn, "row": r}
+    here = (z - 2) * 2 + x
+    over = here + 1 - 2 * x
+    ahead = here + turn // 2
+    slots = (here, over, ahead, over + turn // 2)
+
+    def place(m):
+        return 2 * m + r if m < 4 else 2 * (m - 4) + 1 - r
+
+    def strip_send_copy(slot, m, way):
+        device = (side, turned, mate)[way]
+        p = place(m)
+        src = colf.at[p] if slot == 0 else dcol.at[slots[slot], p]
+        return copy(
+            src, dcol.at[slots[slot], p], strip_send.at[slot, m, way],
+            strip_recv.at[slots[slot], p], device,
+        )
+
+    def strip_wait(g, p):
+        copy(
+            dcol.at[g, p], dcol.at[g, p], strip_send.at[0, 0, 0], strip_recv.at[g, p], mate
+        ).wait_recv()
+
+    def ways(slot, m):
+        if slot == 0:
+            return (0, 1, 2)
+        if slot == 1:
+            return (1, 2) if m % 4 < 2 else (2,)
+        if slot == 2:
+            return (2,) if m % 4 < 2 else (0, 2)
+        return (2,)
+
+    holder = (z >= 2) & (k == r)
+
+    def hand_on(slot, m):
+        if slot > 0:
+            strip_wait(slots[slot], place(m))
+        for way in ways(slot, m):
+            strip_send_copy(slot, m, way).start()
 
     def lane(q, j):
         @pl.when(active(q, j))
@@ -192,6 +234,11 @@
     def base(j):
         return jnp.concatenate([mat[2 * j], mat[2 * j + 1]], axis=0)
 
+    @pl.when(z >= 2)
+    def _():
+        for i in range(4):
+            colf[2 * i + r] = mat[i]
+
     barrier = pltpu.get_barrier_semaphore()
     greet(side)
     greet(mate)
@@ -225,6 +272,8 @@
     @pl.when(z == 1)
     def _():
         lane(1, 2)
+        lane(1, 3)
+        lane(1, 1)
 
     @pl.when(z == 0)
     def _():
@@ -235,49 +284,78 @@
 
     @pl.when(z >= 2)
     def _():
-        col_copy.start()
+        for i in range(4):
+            col_copy(i).start()
+
+    @pl.when(holder)
+    def _():
+        for m in range(4):
+            hand_on(0, m)
 
     @pl.when(z >= 1)
     def _():
         gram[0] = dot3(fac[0].T, fac[0])
-
-    @pl.when(z >= 2)
-    def _():
-        gram[1] = dot3(fac[1].T, fac[1])
-
-    @pl.when(z >= 1)
-    def _():
         lane(0, 1)
         peer_copy(0).start()
 
         @pl.when(z >= 2)
         def _():
-            lane(1, 2)
+            for i in range(4):
+                copy(
+                    mat.at[i], colf.at[2 * i + 1 - r], col_sem.at[i], col_recv.at[i], peer
+                ).wait_recv()
+
+        @pl.when(holder)
+        def _():
+            for m in range(4, 8):
+                hand_on(0, m)
 
         across(0, 1)
         peer_copy(1).start()
-        lane(1, 3)
-        across(1, 2)
+
+        @pl.when(z == 1)
+        def _():
+            lane(0, 2)
+
+        @pl.when(holder)
+        def _():
+            for m in range(4):
+                hand_on(1, m)
+                hand_on(2, m)
+
+        @pl.when(z >= 2)
+        def _():
+            first[...] = dot3(gram[0], colf[0:4].reshape(width, block))
+
         oth_arrived(own)
         oth_copy(0).start()
-        lane(0, 2)
-        lane(1, 1)
-        across(1, 3)
-
-        @pl.when(z >= 2)
-        def _():
-            col_copy.wait_recv()
-            for i in range(4):
-                colf[2 * i + r] = mat[i]
-                colf[2 * i + 1 - r] = colo[i]
-            first[...] = dot3(gram[0], colf[0:4].reshape(width, block))
+
+        @pl.when(z == 1)
+        def _():
+            across(1, 2)
+            across(1, 3)
+            across(1, 1)
+            lane(0, 3)
 
         oth_arrived(beside)
         oth_copy(1).start()
-        across(0, 2)
-        lane(0, 3)
-        across(1, 1)
-        across(0, 3)
+
+        @pl.when(z == 1)
+        def _():
+            across(0, 2)
+
+        @pl.when(holder)
+        def _():
+            for m in range(4, 8):
+                hand_on(1, m)
+                hand_on(2, m)
+            for m in range(8):
+                hand_on(3, m)
+            dcol[here] = colf[...]
+
+        @pl.when(z >= 2)
+        def _():
+            gram[1] = dot3(fac[1].T, fac[1])
 
         complete(0, 1)
         oth_arrived(near)
@@ -287,37 +365,49 @@
                 cross[2 * i + r, :, s * block:(s + 1) * block] = pan[0, s, 2 + i]
                 cross[2 * i + 1 - r, :, s * block:(s + 1) * block] = oth[s, i]
 
-        @pl.when(z == 1)
-        def _():
-            second[...] = -fac[1, pl.ds(pl.multiple_of(own * block, block), block), :].T
-            first[...] = -dot3(cross[...].reshape(width, width).T, second[...])
-
-        @pl.when(z >= 2)
-        def _():
-            put(0, base(0))
-            lower = dot3(cross[...].reshape(width, width), first[...])
-            colf[4:8] = colf[4:8] - lower.reshape(4, block, block)
+    @pl.when(z == 1)
+    def _():
+        second[...] = -fac[1, pl.ds(pl.multiple_of(own * block, block), block), :].T
+        first[...] = -dot3(cross[...].reshape(width, width).T, second[...])
+        first[...] = dot3(gram[0], first[...])
+        across(0, 3)
+        put(0, jnp.zeros((2 * block, block), jnp.float32))
+        for j in (1, 2, 3):
+            complete(1, j)
+            if j > 1:
+                complete(0, j)
+            put(j, -(dot3(rows(0, j), first[...]) + dot3(rows(1, j), second[...])))
+
+    @pl.when(z >= 2)
+    def _():
+        put(0, base(0))
+        lower = colf[4:8].reshape(width, block) - dot3(
+            cross[...].reshape(width, width), first[...]
+        )
+        second[...] = lower
+        for i in range(2):
+            out[2 + i] = second[pl.ds(pl.multiple_of((2 * i + r) * block, block), block), :]
+        second[...] = dot3(gram[1], lower)
+        first[...] = colf[0:4].reshape(width, block) - dot3(
+            cross[...].reshape(width, width).T, second[...]
+        )
+        first[...] = dot3(gram[0], first[...])
+
+        @pl.when(k != r)
+        def _():
+            for g in range(4):
+                for p in range(8):
+                    strip_wait(g, p)
+
+        both = jnp.concatenate([first[...].T, second[...].T], axis=1)
+        for pair in range(2):
+            strips = jnp.concatenate(
+                [dcol[2 * pair + i].reshape(2 * width, block) for i in range(2)], axis=1
+            )
+            update = dot3(both, strips)
             for i in range(2):
-                out[2 + i] = colf[4 + 2 * i + r]
-            second[...] = dot3(gram[1], colf[4:8].reshape(width, block))
-            first[...] = colf[0:4].reshape(width, block) - dot3(
-                cross[...].reshape(width, width).T, second[...]
-            )
-
-        first[...] = dot3(gram[0], first[...])
-        first_value, second_value = first[...], second[...]
-
-        @pl.when(z == 1)
-        def _():
-            put(0, jnp.zeros((2 * block, block), jnp.float32))
-            complete(1, 1)
-            put(1, -(dot3(rows(0, 1), first[...]) + dot3(rows(1, 1), second[...])))
-
-        for j in (2, 3):
-            complete(1, j)
-            complete(0, j)
-            update = dot3(rows(1, j), second_value) + dot3(rows(0, j), first_value)
-            put(j, jnp.where(z >= 2, base(j), 0.0) - update)
+                a = 4 + 2 * pair + i
+                out[a] = mat[a] - update[:, i * block:(i + 1) * block].T
 
     @pl.when(z == 0)
     def _():
@@ -347,7 +437,15 @@
 
     @pl.when(z >= 2)
     def _():
-        col_copy.wait_send()
+        for i in range(4):
+            col_copy(i).wait_send()
+
+    @pl.when(holder)
+    def _():
+        for slot in range(4):
+            for m in range(8):
+                for way in ways(slot, m):
+                    strip_send_copy(slot, m, way).wait_send()
 
 
 def panels(matrix, inverse_factors):
@@ -364,20 +462,22 @@
         scratch_shapes=[
             pltpu.VMEM((2, 4, row_blocks, block, block), jnp.float32),
             pltpu.VMEM((4, 2, block, block), jnp.float32),
-            pltpu.VMEM((4, block, block), jnp.float32),
             pltpu.VMEM((8, block, block), jnp.float32),
+            pltpu.VMEM((4, 8, block, block), jnp.float32),
             pltpu.VMEM((4, block, width), jnp.float32),
             pltpu.VMEM((2, width, width), jnp.float32),
             square,
             square,
             dma((2, 4, 4)),
             dma((4,)),
-            dma,
+            dma((4,)),
             dma((2, 4)),
             dma((2, 4)),
             dma((2, 4, 2)),
             dma((2, 2)),
-            dma,
+            dma((4,)),
+            dma((4, 8)),
+            dma((4, 8, 3)),
         ],
         compiler_params=pltpu.CompilerParams(
             collective_id=0, has_side_effects=True, vmem_limit_bytes=48 * 1024 * 1024

time: 39.7 us -> 40.4 us (1.018)
  the two profiles are of different devices: /device:TPU:28 before, /device:TPU:16 now
where the time goes in v2:
time: 40.4 us; the launch traced here: 40.3 us
  Pallas kernels  36.8 us (91%)
  local copies, waits for them, and re-layouts  3.43 us (8%)
    pallas_call x1, Pallas kernels, panels(): pl.pallas_call(kernel, out_shape=jax.ShapeDtypeStruct((row_blocks, block,...  36.8 us
    unnamed x5, local copies, waits for them, and re-layouts  3.43 us

profile of v2, /device:TPU:16, one launch (start us, length us, event | category | flops | bytes accessed | tf_op | source)
XLA Modules:
  0.0 40.3 jit_solution(548304051887820121)
XLA Ops:
  0.0 0.0 copy-start
  0.0 1.6 %copy-done = f32[2,512,512]{2,1,0:T(8,128)S(1)} copy-done((f32[2,512,512]{2,1,0:T(8,128)S(1)}, f32[2,512,512]{2,1,0:T(8,128)}, u32[]{:S(2)}) %copy-start) | copy-done | bytes 2097176
  1.6 0.0 copy-start.1
  1.6 1.0 %copy-done.1 = f32[8,128,1,128]{3,2,1,0:T(1,128)S(1)} copy-done((f32[8,128,1,128]{3,2,1,0:T(1,128)S(1)}, f32[8,128,1,128]{3,2,1,0:T(1,128)}, u32[]{:S(2)}) %copy-start.1) | copy-done | bytes 524312
  2.6 36.8 %shard_map.28 = f32[8,128,128]{2,1,0:T(8,128)S(1)} custom-call(f32[8,128,128]{2,1,0:T(8,128)S(1)} %bitcast.5, f32[2,512,512]{2,1,0:T(8,128)S(1)} %copy-done), custom_call_target="tpu_custom_call" | custom-call | flops 2000000000 | bytes 4194304 | tf_op jit(solution)/shard_map/pallas_call | solution.py:457
  39.5 0.8 %copy.5 = f32[8,128,1,128]{3,2,1,0:T(1,128)} copy(f32[8,128,1,128]{3,2,1,0:T(1,128)S(1)} %bitcast.4) | data formatting | bytes 1048576
Async XLA Ops:
  0.0 1.6 %copy-start = (f32[2,512,512]{2,1,0:T(8,128)S(1)}, f32[2,512,512]{2,1,0:T(8,128)}, u32[]{:S(2)}) copy-start(f32[2,512,512]{2,1,0:T(8,128)} %fac.1) | copy-start | bytes 6291460
  1.6 1.0 %copy-start.1 = (f32[8,128,1,128]{3,2,1,0:T(1,128)S(1)}, f32[8,128,1,128]{3,2,1,0:T(1,128)}, u32[]{:S(2)}) copy-start(f32[8,128,1,128]{3,2,1,0:T(1,128)} %param.2) | copy-start | bytes 1572868

commit v3 on v2

--- a/solution.py
+++ b/solution.py
@@ -80,8 +80,8 @@
 
 
 def kernel(
-    mat, fac, out, pan, oth, colf, dcol, cross, gram, first, second,
-    recv, oth_recv, col_recv, up_sem, side_sem, mate_sem, peer_sem, col_sem, strip_recv, strip_send,
+    mat_hbm, fac_hbm, out, mat, fac, pan, oth, colf, dcol, cross, gram, first, second,
+    recv, oth_recv, col_recv, up_sem, side_sem, mate_sem, peer_sem, col_sem, strip_recv, strip_send, load_sem,
 ):
     c = lax.axis_index("col")
     r = lax.axis_index("row")
@@ -166,7 +166,8 @@
     def strip_send_copy(slot, m, way):
         device = (side, turned, mate)[way]
         p = place(m)
-        src = colf.at[p] if slot == 0 else dcol.at[slots[slot], p]
+        from_column = slot == 0 and (m % 2 == 0 or way == 2)
+        src = colf.at[p] if from_column else dcol.at[slots[slot], p]
         return copy(
             src, dcol.at[slots[slot], p], strip_send.at[slot, m, way],
             strip_recv.at[slots[slot], p], device,
@@ -187,12 +188,22 @@
         return (2,)
 
     holder = (z >= 2) & (k == r)
+    helper = (z >= 2) & (k != r)
+
+    def carried(cases):
+        for even, condition in ((True, holder), (False, helper)):
+            @pl.when(condition)
+            def _():
+                for slot, m in cases:
+                    if (m % 2 == 0) == even:
+                        hand_on(slot, m)
 
     def hand_on(slot, m):
-        if slot > 0:
+        if slot > 0 or m % 2:
             strip_wait(slots[slot], place(m))
         for way in ways(slot, m):
-            strip_send_copy(slot, m, way).start()
+            if slot > 0 or m % 2 == 0 or way < 2:
+                strip_send_copy(slot, m, way).start()
 
     def lane(q, j):
         @pl.when(active(q, j))
@@ -234,10 +245,10 @@
     def base(j):
         return jnp.concatenate([mat[2 * j], mat[2 * j + 1]], axis=0)
 
-    @pl.when(z >= 2)
-    def _():
-        for i in range(4):
-            colf[2 * i + r] = mat[i]
+    mat_load = pltpu.make_async_copy(mat_hbm, mat, load_sem.at[0])
+    fac_load = pltpu.make_async_copy(fac_hbm, fac, load_sem.at[1])
+    mat_load.start()
+    fac_load.start()
 
     barrier = pltpu.get_barrier_semaphore()
     greet(side)
@@ -252,6 +263,13 @@
     def _():
         greet(down)
 
+    mat_load.wait()
+
+    @pl.when(z >= 2)
+    def _():
+        for i in range(4):
+            colf[2 * i + r] = mat[i]
+
     for q in range(2):
         @pl.when(z == q)
         def _():
@@ -289,8 +307,11 @@
 
     @pl.when(holder)
     def _():
-        for m in range(4):
-            hand_on(0, m)
+        for m in (1, 3):
+            strip_send_copy(0, m, 2).start()
+
+    carried([(0, m) for m in range(4)])
+    fac_load.wait()
 
     @pl.when(z >= 1)
     def _():
@@ -307,8 +328,10 @@
 
         @pl.when(holder)
         def _():
-            for m in range(4, 8):
-                hand_on(0, m)
+            for m in (5, 7):
+                strip_send_copy(0, m, 2).start()
+
+        carried([(0, m) for m in range(4, 8)])
 
         across(0, 1)
         peer_copy(1).start()
@@ -317,14 +340,11 @@
         def _():
             lane(0, 2)
 
-        @pl.when(holder)
-        def _():
-            for m in range(4):
-                hand_on(1, m)
-                hand_on(2, m)
+        carried([(slot, m) for m in range(4) for slot in (1, 2)])
 
         @pl.when(z >= 2)
         def _():
+            gram[1] = dot3(fac[1].T, fac[1])
             first[...] = dot3(gram[0], colf[0:4].reshape(width, block))
 
         oth_arrived(own)
@@ -344,18 +364,12 @@
         def _():
             across(0, 2)
 
+        carried([(slot, m) for m in range(4, 8) for slot in (1, 2)])
+        carried([(3, m) for m in range(8)])
+
         @pl.when(holder)
         def _():
-            for m in range(4, 8):
-                hand_on(1, m)
-                hand_on(2, m)
-            for m in range(8):
-                hand_on(3, m)
             dcol[here] = colf[...]
-
-        @pl.when(z >= 2)
-        def _():
-            gram[1] = dot3(fac[1].T, fac[1])
 
         complete(0, 1)
         oth_arrived(near)
@@ -393,11 +407,17 @@
         )
         first[...] = dot3(gram[0], first[...])
 
+        @pl.when(k == r)
+        def _():
+            for slot in (1, 2, 3):
+                for m in (1, 3, 5, 7):
+                    strip_wait(slots[slot], place(m))
+
         @pl.when(k != r)
         def _():
-            for g in range(4):
-                for p in range(8):
-                    strip_wait(g, p)
+            for slot in range(4):
+                for m in (0, 2, 4, 6):
+                    strip_wait(slots[slot], place(m))
 
         both = jnp.concatenate([first[...].T, second[...].T], axis=1)
         for pair in range(2):
@@ -440,12 +460,15 @@
         for i in range(4):
             col_copy(i).wait_send()
 
-    @pl.when(holder)
-    def _():
-        for slot in range(4):
-            for m in range(8):
-                for way in ways(slot, m):
-                    strip_send_copy(slot, m, way).wait_send()
+    for even, condition in ((True, holder), (False, helper)):
+        @pl.when(condition)
+        def _():
+            for slot in range(4):
+                for m in range(8):
+                    for way in ways(slot, m):
+                        shared = slot == 0 and m % 2 == 1 and way == 2
+                        if even == (m % 2 == 0 or shared):
+                            strip_send_copy(slot, m, way).wait_send()
 
 
 def panels(matrix, inverse_factors):
@@ -457,9 +480,11 @@
     result = pl.pallas_call(
         kernel,
         out_shape=jax.ShapeDtypeStruct((row_blocks, block, block), jnp.float32),
-        in_specs=[vmem, vmem],
+        in_specs=[pl.BlockSpec(memory_space=pltpu.HBM)] * 2,
         out_specs=vmem,
         scratch_shapes=[
+            pltpu.VMEM((row_blocks, block, block), jnp.float32),
+            pltpu.VMEM((2, width, width), jnp.float32),
             pltpu.VMEM((2, 4, row_blocks, block, block), jnp.float32),
             pltpu.VMEM((4, 2, block, block), jnp.float32),
             pltpu.VMEM((8, block, block), jnp.float32),
@@ -478,6 +503,7 @@
             dma((4,)),
             dma((4, 8)),
             dma((4, 8, 3)),
+            dma((2,)),
         ],
         compiler_params=pltpu.CompilerParams(
             collective_id=0, has_side_effects=True, vmem_limit_bytes=48 * 1024 * 1024

time: 40.4 us -> 36.6 us (0.906)
  the two profiles are of different devices: /device:TPU:16 before, /device:TPU:20 now
where the time goes in v3:
time: 36.6 us; the launch traced here: 36.4 us
  Pallas kernels  32.9 us (90%)
  local copies, waits for them, and re-layouts  3.43 us (9%)
    pallas_call x1, Pallas kernels, panels(): pl.pallas_call(kernel, out_shape=jax.ShapeDtypeStruct((row_blocks, block,...  32.9 us
    unnamed x5, local copies, waits for them, and re-layouts  3.43 us

profile of v3, /device:TPU:20, one launch (start us, length us, event | category | flops | bytes accessed | tf_op | source)
XLA Modules:
  0.0 36.4 jit_solution(2583988477347562809)
XLA Ops:
  0.0 0.0 copy-start
  0.0 1.6 %copy-done = f32[2,512,512]{2,1,0:T(8,128)S(1)} copy-done((f32[2,512,512]{2,1,0:T(8,128)S(1)}, f32[2,512,512]{2,1,0:T(8,128)}, u32[]{:S(2)}) %copy-start) | copy-done | bytes 2097176
  1.6 0.0 copy-start.1
  1.6 1.0 %copy-done.1 = f32[8,128,1,128]{3,2,1,0:T(1,128)S(1)} copy-done((f32[8,128,1,128]{3,2,1,0:T(1,128)S(1)}, f32[8,128,1,128]{3,2,1,0:T(1,128)}, u32[]{:S(2)}) %copy-start.1) | copy-done | bytes 524312
  2.6 32.9 %shard_map.28 = f32[8,128,128]{2,1,0:T(8,128)S(1)} custom-call(f32[8,128,128]{2,1,0:T(8,128)S(1)} %bitcast.5, f32[2,512,512]{2,1,0:T(8,128)S(1)} %copy-done), custom_call_target="tpu_custom_call" | custom-call | flops 2000000000 | bytes 4194304 | tf_op jit(solution)/shard_map/pallas_call | solution.py:480
  35.6 0.8 %copy.5 = f32[8,128,1,128]{3,2,1,0:T(1,128)} copy(f32[8,128,1,128]{3,2,1,0:T(1,128)S(1)} %bitcast.4) | data formatting | bytes 1048576
Async XLA Ops:
  0.0 1.6 %copy-start = (f32[2,512,512]{2,1,0:T(8,128)S(1)}, f32[2,512,512]{2,1,0:T(8,128)}, u32[]{:S(2)}) copy-start(f32[2,512,512]{2,1,0:T(8,128)} %fac_hbm.1) | copy-start | bytes 6291460
  1.6 1.0 %copy-start.1 = (f32[8,128,1,128]{3,2,1,0:T(1,128)S(1)}, f32[8,128,1,128]{3,2,1,0:T(1,128)}, u32[]{:S(2)}) copy-start(f32[8,128,1,128]{3,2,1,0:T(1,128)} %param.2) | copy-start | bytes 1572868

commit v4 on v3

--- a/solution.py
+++ b/solution.py
@@ -163,11 +163,10 @@
     def place(m):
         return 2 * m + r if m < 4 else 2 * (m - 4) + 1 - r
 
-    def strip_send_copy(slot, m, way):
+    def strip_send_copy(slot, m, way, relayed=False):
         device = (side, turned, mate)[way]
         p = place(m)
-        from_column = slot == 0 and (m % 2 == 0 or way == 2)
-        src = colf.at[p] if from_column else dcol.at[slots[slot], p]
+        src = colf.at[p] if slot == 0 and not relayed else dcol.at[slots[slot], p]
         return copy(
             src, dcol.at[slots[slot], p], strip_send.at[slot, m, way],
             strip_recv.at[slots[slot], p], device,
@@ -188,22 +187,24 @@
         return (2,)
 
     holder = (z >= 2) & (k == r)
-    helper = (z >= 2) & (k != r)
+    lead = holder & (k == 1)
+    giver = holder & (k == 0)
+    relay = (z >= 2) & (k == 1) & (r == 0)
+    taker = (z >= 2) & (k == 0) & (r == 1)
+
+    def hand_on(slot, m, relayed):
+        if slot > 0 or relayed:
+            strip_wait(slots[slot], place(m))
+        for way in ways(slot, m):
+            if slot > 0 or not relayed or way < 2:
+                strip_send_copy(slot, m, way, relayed).start()
 
     def carried(cases):
-        for even, condition in ((True, holder), (False, helper)):
+        for relayed, condition in ((False, lead), (True, relay)):
             @pl.when(condition)
             def _():
                 for slot, m in cases:
-                    if (m % 2 == 0) == even:
-                        hand_on(slot, m)
-
-    def hand_on(slot, m):
-        if slot > 0 or m % 2:
-            strip_wait(slots[slot], place(m))
-        for way in ways(slot, m):
-            if slot > 0 or m % 2 == 0 or way < 2:
-                strip_send_copy(slot, m, way).start()
+                    hand_on(slot, m, relayed)
 
     def lane(q, j):
         @pl.when(active(q, j))
@@ -305,9 +306,9 @@
         for i in range(4):
             col_copy(i).start()
 
-    @pl.when(holder)
-    def _():
-        for m in (1, 3):
+    @pl.when(giver)
+    def _():
+        for m in range(4):
             strip_send_copy(0, m, 2).start()
 
     carried([(0, m) for m in range(4)])
@@ -316,8 +317,10 @@
     @pl.when(z >= 1)
     def _():
         gram[0] = dot3(fac[0].T, fac[0])
-        lane(0, 1)
-        peer_copy(0).start()
+        @pl.when(z <= 2)
+        def _():
+            lane(0, 1)
+            peer_copy(0).start()
 
         @pl.when(z >= 2)
         def _():
@@ -326,12 +329,18 @@
                     mat.at[i], colf.at[2 * i + 1 - r], col_sem.at[i], col_recv.at[i], peer
                 ).wait_recv()
 
-        @pl.when(holder)
-        def _():
-            for m in (5, 7):
+        @pl.when(giver)
+        def _():
+            for m in range(4, 8):
                 strip_send_copy(0, m, 2).start()
 
         carried([(0, m) for m in range(4, 8)])
+        carried([(slot, m) for m in range(4) for slot in (1, 2)])
+
+        @pl.when(z == 3)
+        def _():
+            lane(0, 1)
+            peer_copy(0).start()
 
         across(0, 1)
         peer_copy(1).start()
@@ -340,7 +349,6 @@
         def _():
             lane(0, 2)
 
-        carried([(slot, m) for m in range(4) for slot in (1, 2)])
 
         @pl.when(z >= 2)
         def _():
@@ -407,17 +415,16 @@
         )
         first[...] = dot3(gram[0], first[...])
 
-        @pl.when(k == r)
+        @pl.when(k == 0)
         def _():
             for slot in (1, 2, 3):
-                for m in (1, 3, 5, 7):
+                for m in range(8):
                     strip_wait(slots[slot], place(m))
 
-        @pl.when(k != r)
-        def _():
-            for slot in range(4):
-                for m in (0, 2, 4, 6):
-                    strip_wait(slots[slot], place(m))
+        @pl.when(taker)
+        def _():
+            for m in range(8):
+                strip_wait(here, place(m))
 
         both = jnp.concatenate([first[...].T, second[...].T], axis=1)
         for pair in range(2):
@@ -460,15 +467,19 @@
         for i in range(4):
             col_copy(i).wait_send()
 
-    for even, condition in ((True, holder), (False, helper)):
+    for relayed, condition in ((False, lead), (True, relay)):
         @pl.when(condition)
         def _():
             for slot in range(4):
                 for m in range(8):
                     for way in ways(slot, m):
-                        shared = slot == 0 and m % 2 == 1 and way == 2
-                        if even == (m % 2 == 0 or shared):
-                            strip_send_copy(slot, m, way).wait_send()
+                        if slot > 0 or not relayed or way < 2:
+                            strip_send_copy(slot, m, way, relayed).wait_send()
+
+    @pl.when(giver)
+    def _():
+        for m in range(8):
+            strip_send_copy(0, m, 2).wait_send()
 
 
 def panels(matrix, inverse_factors):

time: 36.6 us -> 36.5 us (level)
  the two profiles are of different devices: /device:TPU:20 before, /device:TPU:23 now
where the time goes in v4:
time: 36.5 us; the launch traced here: 36.3 us
  Pallas kernels  32.9 us (90%)
  local copies, waits for them, and re-layouts  3.43 us (9%)
    pallas_call x1, Pallas kernels, panels(): pl.pallas_call(kernel, out_shape=jax.ShapeDtypeStruct((row_blocks, block,...  32.9 us
    unnamed x5, local copies, waits for them, and re-layouts  3.43 us

profile of v4, /device:TPU:23, one launch (start us, length us, event | category | flops | bytes accessed | tf_op | source)
XLA Modules:
  0.0 36.3 jit_solution(17304384708139487133)
XLA Ops:
  0.0 0.0 copy-start
  0.0 1.6 %copy-done = f32[2,512,512]{2,1,0:T(8,128)S(1)} copy-done((f32[2,512,512]{2,1,0:T(8,128)S(1)}, f32[2,512,512]{2,1,0:T(8,128)}, u32[]{:S(2)}) %copy-start) | copy-done | bytes 2097176
  1.6 0.0 copy-start.1
  1.6 1.0 %copy-done.1 = f32[8,128,1,128]{3,2,1,0:T(1,128)S(1)} copy-done((f32[8,128,1,128]{3,2,1,0:T(1,128)S(1)}, f32[8,128,1,128]{3,2,1,0:T(1,128)}, u32[]{:S(2)}) %copy-start.1) | copy-done | bytes 524312
  2.6 32.9 %shard_map.28 = f32[8,128,128]{2,1,0:T(8,128)S(1)} custom-call(f32[8,128,128]{2,1,0:T(8,128)S(1)} %bitcast.5, f32[2,512,512]{2,1,0:T(8,128)S(1)} %copy-done), custom_call_target="tpu_custom_call" | custom-call | flops 2000000000 | bytes 4194304 | tf_op jit(solution)/shard_map/pallas_call | solution.py:491
  35.5 0.8 %copy.5 = f32[8,128,1,128]{3,2,1,0:T(1,128)} copy(f32[8,128,1,128]{3,2,1,0:T(1,128)S(1)} %bitcast.4) | data formatting | bytes 1048576
Async XLA Ops:
  0.0 1.6 %copy-start = (f32[2,512,512]{2,1,0:T(8,128)S(1)}, f32[2,512,512]{2,1,0:T(8,128)}, u32[]{:S(2)}) copy-start(f32[2,512,512]{2,1,0:T(8,128)} %fac_hbm.1) | copy-start | bytes 6291460
  1.6 1.0 %copy-start.1 = (f32[8,128,1,128]{3,2,1,0:T(1,128)S(1)}, f32[8,128,1,128]{3,2,1,0:T(1,128)}, u32[]{:S(2)}) copy-start(f32[8,128,1,128]{3,2,1,0:T(1,128)} %param.2) | copy-start | bytes 1572868

commit v5 on v4

--- a/solution.py
+++ b/solution.py
@@ -342,6 +342,7 @@
             lane(0, 1)
             peer_copy(0).start()
 
+        carried([(slot, m) for m in range(4, 8) for slot in (1, 2)])
         across(0, 1)
         peer_copy(1).start()
 
@@ -355,6 +356,7 @@
             gram[1] = dot3(fac[1].T, fac[1])
             first[...] = dot3(gram[0], colf[0:4].reshape(width, block))
 
+        carried([(3, m) for m in range(4)])
         oth_arrived(own)
         oth_copy(0).start()
 
@@ -372,8 +374,7 @@
         def _():
             across(0, 2)
 
-        carried([(slot, m) for m in range(4, 8) for slot in (1, 2)])
-        carried([(3, m) for m in range(8)])
+        carried([(3, m) for m in range(4, 8)])
 
         @pl.when(holder)
         def _():

time: 36.5 us -> 35.4 us (0.970)
  the two profiles are of different devices: /device:TPU:23 before, /device:TPU:25 now
where the time goes in v5:
time: 35.4 us; the launch traced here: 35.3 us
  Pallas kernels  31.8 us (90%)
  local copies, waits for them, and re-layouts  3.43 us (10%)
    pallas_call x1, Pallas kernels, panels(): pl.pallas_call(kernel, out_shape=jax.ShapeDtypeStruct((row_blocks, block,...  31.8 us
    unnamed x5, local copies, waits for them, and re-layouts  3.43 us

profile of v5, /device:TPU:25, one launch (start us, length us, event | category | flops | bytes accessed | tf_op | source)
XLA Modules:
  0.0 35.3 jit_solution(12035592031330080123)
XLA Ops:
  0.0 0.0 copy-start
  0.0 1.6 %copy-done = f32[2,512,512]{2,1,0:T(8,128)S(1)} copy-done((f32[2,512,512]{2,1,0:T(8,128)S(1)}, f32[2,512,512]{2,1,0:T(8,128)}, u32[]{:S(2)}) %copy-start) | copy-done | bytes 2097176
  1.6 0.0 copy-start.1
  1.6 1.0 %copy-done.1 = f32[8,128,1,128]{3,2,1,0:T(1,128)S(1)} copy-done((f32[8,128,1,128]{3,2,1,0:T(1,128)S(1)}, f32[8,128,1,128]{3,2,1,0:T(1,128)}, u32[]{:S(2)}) %copy-start.1) | copy-done | bytes 524312
  2.6 31.8 %shard_map.28 = f32[8,128,128]{2,1,0:T(8,128)S(1)} custom-call(f32[8,128,128]{2,1,0:T(8,128)S(1)} %bitcast.5, f32[2,512,512]{2,1,0:T(8,128)S(1)} %copy-done), custom_call_target="tpu_custom_call" | custom-call | flops 2000000000 | bytes 4194304 | tf_op jit(solution)/shard_map/pallas_call | solution.py:492
  34.5 0.8 %copy.5 = f32[8,128,1,128]{3,2,1,0:T(1,128)} copy(f32[8,128,1,128]{3,2,1,0:T(1,128)S(1)} %bitcast.4) | data formatting | bytes 1048576
Async XLA Ops:
  0.0 1.6 %copy-start = (f32[2,512,512]{2,1,0:T(8,128)S(1)}, f32[2,512,512]{2,1,0:T(8,128)}, u32[]{:S(2)}) copy-start(f32[2,512,512]{2,1,0:T(8,128)} %fac_hbm.1) | copy-start | bytes 6291460
  1.6 1.0 %copy-start.1 = (f32[8,128,1,128]{3,2,1,0:T(1,128)S(1)}, f32[8,128,1,128]{3,2,1,0:T(1,128)}, u32[]{:S(2)}) copy-start(f32[8,128,1,128]{3,2,1,0:T(1,128)} %param.2) | copy-start | bytes 1572868

commit v6 on v5

--- a/solution.py
+++ b/solution.py
@@ -316,11 +316,12 @@
 
     @pl.when(z >= 1)
     def _():
-        gram[0] = dot3(fac[0].T, fac[0])
         @pl.when(z <= 2)
         def _():
             lane(0, 1)
             peer_copy(0).start()
+
+        gram[0] = dot3(fac[0].T, fac[0])
 
         @pl.when(z >= 2)
         def _():

time: 35.4 us -> 35.4 us (level)
  no operation moved by 1% of the time
where the time goes in v6:
time: 35.4 us; the launch traced here: 35.3 us
  Pallas kernels  31.8 us (90%)
  local copies, waits for them, and re-layouts  3.43 us (10%)
    pallas_call x1, Pallas kernels, panels(): pl.pallas_call(kernel, out_shape=jax.ShapeDtypeStruct((row_blocks, block,...  31.8 us
    unnamed x5, local copies, waits for them, and re-layouts  3.43 us

profile of v6, /device:TPU:25, one launch (start us, length us, event | category | flops | bytes accessed | tf_op | source)
XLA Modules:
  0.0 35.3 jit_solution(11987634625517727097)
XLA Ops:
  0.0 0.0 copy-start
  0.0 1.6 %copy-done = f32[2,512,512]{2,1,0:T(8,128)S(1)} copy-done((f32[2,512,512]{2,1,0:T(8,128)S(1)}, f32[2,512,512]{2,1,0:T(8,128)}, u32[]{:S(2)}) %copy-start) | copy-done | bytes 2097176
  1.6 0.0 copy-start.1
  1.6 1.0 %copy-done.1 = f32[8,128,1,128]{3,2,1,0:T(1,128)S(1)} copy-done((f32[8,128,1,128]{3,2,1,0:T(1,128)S(1)}, f32[8,128,1,128]{3,2,1,0:T(1,128)}, u32[]{:S(2)}) %copy-start.1) | copy-done | bytes 524312
  2.6 31.8 %shard_map.28 = f32[8,128,128]{2,1,0:T(8,128)S(1)} custom-call(f32[8,128,128]{2,1,0:T(8,128)S(1)} %bitcast.5, f32[2,512,512]{2,1,0:T(8,128)S(1)} %copy-done), custom_call_target="tpu_custom_call" | custom-call | flops 2000000000 | bytes 4194304 | tf_op jit(solution)/shard_map/pallas_call | solution.py:493
  34.5 0.8 %copy.5 = f32[8,128,1,128]{3,2,1,0:T(1,128)} copy(f32[8,128,1,128]{3,2,1,0:T(1,128)S(1)} %bitcast.4) | data formatting | bytes 1048576
Async XLA Ops:
  0.0 1.6 %copy-start = (f32[2,512,512]{2,1,0:T(8,128)S(1)}, f32[2,512,512]{2,1,0:T(8,128)}, u32[]{:S(2)}) copy-start(f32[2,512,512]{2,1,0:T(8,128)} %fac_hbm.1) | copy-start | bytes 6291460
  1.6 1.0 %copy-start.1 = (f32[8,128,1,128]{3,2,1,0:T(1,128)S(1)}, f32[8,128,1,128]{3,2,1,0:T(1,128)}, u32[]{:S(2)}) copy-start(f32[8,128,1,128]{3,2,1,0:T(1,128)} %param.2) | copy-start | bytes 1572868

commit v7 on v6

--- a/solution.py
+++ b/solution.py
@@ -336,12 +336,13 @@
                 strip_send_copy(0, m, 2).start()
 
         carried([(0, m) for m in range(4, 8)])
-        carried([(slot, m) for m in range(4) for slot in (1, 2)])
 
         @pl.when(z == 3)
         def _():
             lane(0, 1)
             peer_copy(0).start()
+
+        carried([(slot, m) for m in range(4) for slot in (1, 2)])
 
         carried([(slot, m) for m in range(4, 8) for slot in (1, 2)])
         across(0, 1)

time: 35.4 us -> 35.4 us (level)
  no operation moved by 1% of the time
where the time goes in v7:
time: 35.4 us; the launch traced here: 35.3 us
  Pallas kernels  31.8 us (90%)
  local copies, waits for them, and re-layouts  3.43 us (10%)
    pallas_call x1, Pallas kernels, panels(): pl.pallas_call(kernel, out_shape=jax.ShapeDtypeStruct((row_blocks, block,...  31.8 us
    unnamed x5, local copies, waits for them, and re-layouts  3.43 us

profile of v7, /device:TPU:25, one launch (start us, length us, event | category | flops | bytes accessed | tf_op | source)
XLA Modules:
  0.0 35.3 jit_solution(5008828744690944233)
XLA Ops:
  0.0 0.0 copy-start
  0.0 1.6 %copy-done = f32[2,512,512]{2,1,0:T(8,128)S(1)} copy-done((f32[2,512,512]{2,1,0:T(8,128)S(1)}, f32[2,512,512]{2,1,0:T(8,128)}, u32[]{:S(2)}) %copy-start) | copy-done | bytes 2097176
  1.6 0.0 copy-start.1
  1.6 1.0 %copy-done.1 = f32[8,128,1,128]{3,2,1,0:T(1,128)S(1)} copy-done((f32[8,128,1,128]{3,2,1,0:T(1,128)S(1)}, f32[8,128,1,128]{3,2,1,0:T(1,128)}, u32[]{:S(2)}) %copy-start.1) | copy-done | bytes 524312
  2.6 31.8 %shard_map.28 = f32[8,128,128]{2,1,0:T(8,128)S(1)} custom-call(f32[8,128,128]{2,1,0:T(8,128)S(1)} %bitcast.5, f32[2,512,512]{2,1,0:T(8,128)S(1)} %copy-done), custom_call_target="tpu_custom_call" | custom-call | flops 2000000000 | bytes 4194304 | tf_op jit(solution)/shard_map/pallas_call | solution.py:494
  34.5 0.8 %copy.5 = f32[8,128,1,128]{3,2,1,0:T(1,128)} copy(f32[8,128,1,128]{3,2,1,0:T(1,128)S(1)} %bitcast.4) | data formatting | bytes 1048576
Async XLA Ops:
  0.0 1.6 %copy-start = (f32[2,512,512]{2,1,0:T(8,128)S(1)}, f32[2,512,512]{2,1,0:T(8,128)}, u32[]{:S(2)}) copy-start(f32[2,512,512]{2,1,0:T(8,128)} %fac_hbm.1) | copy-start | bytes 6291460
  1.6 1.0 %copy-start.1 = (f32[8,128,1,128]{3,2,1,0:T(1,128)S(1)}, f32[8,128,1,128]{3,2,1,0:T(1,128)}, u32[]{:S(2)}) copy-start(f32[8,128,1,128]{3,2,1,0:T(1,128)} %param.2) | copy-start | bytes 1572868
